TPU v7x, 256 devices: a whole 4x4x8 slice. The times are simulated.
256 devices in a mesh: cam: 64 (over z, y, core), rows: 4 (over x).
Axes of the slice: x: 4, y: 4, z: 8, core: 2. Of those that a mesh axis runs over, the one named last changes fastest.
Arguments:
- images: bfloat16 [64, 3, 32, 256], P('cam', None, 'rows'), may hold values from -6 to 6
- neighbor_ids: int32 [64, 6], P('cam'), may hold values from -1 to 63, as said below
- neighbor_count: int32 [64], P('cam'), may hold values from 2 to 6, as said below
- offsets: int32 [64, 6], P('cam'), may hold values from -1 to 1
- w_first: bfloat16 [64, 27], replicated, may hold values from -1.25 to 1.25
- w_second: bfloat16 [64, 64], replicated, may hold values from -0.75 to 0.75
- kernel_one: float32 [27], replicated, may hold values from -1.2 to 1.2
- kernel_two: float32 [27], replicated, may hold values from -1.2 to 1.2
- biases: float32 [2], replicated, may hold values from -0.6 to 0.6
Outputs:
- cost_volume: bfloat16 [64, 192, 32, 256], P('cam', None, 'rows')
Inputs may be any that keep to these rules, and one draw needn't show every extreme that they name: For k < neighbor_count[i], neighbor_ids[i, k] is a camera at cycle distance 1 to 3 from camera i (modulo 64), no camera twice in one list; the remaining slots hold -1. `neighbor_count`: some camera has 6 neighbours and some has 2.
All inputs are finite; a program needn't handle non-finite values.
Results may differ from a plain program's by a relative error of at most 0.012.
Values may be sent and summed in bfloat16 or wider, within the bound.
No kernel may reach another device: no remote copies, remote signals or barrier semaphores. Data moves between devices by JAX's collectives and lax.ppermute only.
A program may use at most 128 MiB of HBM per device.

v0:
```python
import jax
import jax.numpy as jnp
from jax import lax
from jax.experimental import pallas as pl
from jax.experimental.pallas import tpu as pltpu
from jax.sharding import PartitionSpec as P

C = 64
D = 192
W = 256
NBR = 6
CAMS = 64
H = 32
BAND = 8
ROWS = BAND + 4
TALL = BAND + 8
TAPS = 9 * TALL
BLOCKS = D // 8
F32 = jnp.float32
BF16 = jnp.bfloat16


def iota(shape, axis):
    return lax.broadcasted_iota(jnp.int32, shape, axis)


def one_hot(condition):
    return condition.astype(F32).astype(BF16)


def spread_first(w_first, wide):
    shape = (32, 256)
    tap, k = iota(shape, 0), iota(shape, 1)
    q = k >> 4
    p = (q * 11) >> 5
    for y in range(ROWS):
        a = (k & 15) - y - 1
        chosen = (a >= 0) & (a <= 2) & (q < 9) & (tap == 6 * p + q + 3 * a)
        taps = lax.dot_general(
            w_first, one_hot(chosen), (((0,), (0,)), ((), ())), preferred_element_type=F32
        )
        wide[64 * y : 64 * y + 64, :] = taps[:, :TAPS].astype(BF16)


def fill_taps(a, b, taps_ref, store):
    masks = [[(a == i) & (b == j) for j in range(3)] for i in range(3)]
    for e in range(3):
        filled = jnp.zeros(a.shape, F32)
        for i in range(3):
            for j in range(3):
                filled = jnp.where(masks[i][j], taps_ref[9 * i + 3 * j + e], filled)
        high = filled.astype(BF16)
        store(e, high, (filled - high.astype(F32)).astype(BF16))


def spread_filters(k_one, k_two, one, two):
    shape = (40, 192)
    m, k = iota(shape, 0), iota(shape, 1)
    a = 8 * (k >> 6) - 7 + (k & 7) - (m & 7)
    b = ((k >> 3) & 7) - (m >> 3)
    for half in range(2):
        parts = [[], []]

        def keep(e, high, low):
            parts[0].append(high.astype(F32))
            parts[1].append(low.astype(F32))

        fill_taps(a, b - half, k_one, keep)
        for n in range(2):
            one[half, n] = jnp.concatenate(parts[n], axis=0).astype(BF16)
    shape = (64, 240)
    m, k = iota(shape, 0), iota(shape, 1)
    q = k >> 3
    t = (q >= 10).astype(jnp.int32) + (q >= 20).astype(jnp.int32)
    a = 8 * t - 7 + (k & 7) - (m >> 3)
    b = (q - 10 * t) - (m & 7)

    def save(e, high, low):
        two[0, 64 * e : 64 * e + 64] = high
        two[1, 64 * e : 64 * e + 64] = low

    fill_taps(a, b, k_two, save)


def turned_columns(value):
    mirror = one_hot(iota((W, W), 0) + iota((W, W), 1) == W - 1)
    return jnp.dot(value, mirror, preferred_element_type=F32)


def columns_of(picture_of, shift):
    lane = iota((TALL, W), 1)
    parts = []
    for p in range(3):
        rows = picture_of(p).astype(F32)
        if shift is not None:
            rows = pltpu.roll(rows, jnp.where(shift > 0, TALL - shift, -shift), axis=0)
        sides = [
            jnp.where(lane == 0, 0.0, pltpu.roll(rows, 1, axis=1)),
            rows,
            jnp.where(lane == W - 1, 0.0, pltpu.roll(rows, W - 1, axis=1)),
        ]
        parts += sides if shift is None else sides[::-1]
    return jnp.concatenate(parts, axis=0).astype(BF16)


def side_sum(parts):
    lane = iota(parts[0].shape, 1)
    left = jnp.where(lane == 0, 0.0, pltpu.roll(parts[0], 1, axis=1))
    right = jnp.where(lane == W - 1, 0.0, pltpu.roll(parts[2], W - 1, axis=1))
    return left + parts[1] + right


def features(columns, wide, w_second, group, top, listed):
    hidden = jnp.dot(wide[256 * group : 256 * group + 256, :], columns, preferred_element_type=F32)
    found = []
    for q in range(4):
        row = top + 4 * group + q
        keep = jnp.where((row >= 0) & (row < H) & listed, 1.0, 0.0)
        part = jnp.maximum(hidden[64 * q : 64 * q + 64], 0.0) * keep
        found.append(jnp.dot(w_second, part.astype(BF16), preferred_element_type=F32))
    return found


def read_table(table):
    value = [table[n] for n in range(15)]
    return value[0:2], value[2:8], value[14:15], value[8:14]


def wrapped(camera):
    return (camera + CAMS) & (CAMS - 1)


def neighbour_features(others, pictures, wide, w_second, place, ids, count, offsets, right):
    number = len(others)
    mirrored = turned_columns(pictures.reshape(number * 3 * TALL, W))
    for index, other in enumerate(others):
        shift, listed = jnp.int32(0), jnp.bool_(False)
        for slot in range(NBR):
            here = (ids[slot] == other) & (slot < count[0])
            shift = jnp.where(here, offsets[slot], shift)
            listed = listed | here
        columns = columns_of(
            lambda p: mirrored[(3 * index + p) * TALL : (3 * index + p + 1) * TALL], shift
        )
        for group in range(3):
            parts = features(columns, wide, w_second, group, place[1] - 2 + shift, listed)
            for q, part in enumerate(parts):
                at = 256 * group + 64 * q
                right[index, at : at + 64] = part.astype(BF16)


def correlated(left, right, row, upper, lower):
    pair, base = row // 2, W * (row % 2)
    top = left[pair, base : base + 128]
    bottom = left[pair, base + 128 : base + 256]
    for index in range(right.shape[0]):
        other = right[index, 128 * pair : 128 * pair + 128, :]
        a = jnp.maximum(jnp.dot(top, other[:, 128:], preferred_element_type=F32), 0.0)
        b = jnp.maximum(jnp.dot(bottom, other, preferred_element_type=F32), 0.0)
        upper = a if upper is None else upper + a
        lower = b if lower is None else lower + b
    return upper, lower


def early_kernel(table, weights, pictures, left, upper, lower, wide, right):
    place, ids, count, offsets = read_table(table)
    columns = columns_of(lambda p: pictures[0, p], None)
    w_second = weights[0:64]
    spread_first(weights[64:96], wide)
    lane = iota((W, 128), 1)
    for group in range(3):
        found = features(columns, wide, w_second, group, place[1] - 2, True)
        for half in range(2):
            pair = jnp.concatenate(found[2 * half : 2 * half + 2], axis=0).T
            left[2 * group + half, 0:W] = jnp.where(lane < 64, pair, 0.0).astype(BF16)
            left[2 * group + half, W : 2 * W] = jnp.where(lane >= 64, pair, 0.0).astype(BF16)
    neighbour_features(
        [place[0] ^ 1], pictures[1], wide, w_second, place, ids, count, offsets, right
    )
    for row in range(ROWS):
        upper[row], lower[row] = correlated(left, right, row, None, None)


def late_kernel(
    table, floats, weights, pictures, left, upper_sum, lower_sum, wide, out, one, two, right, vol, smooth, result, sems
):
    place, ids, count, offsets = read_table(table)
    k_one = [floats[n] for n in range(27)]
    k_two = [floats[27 + n] for n in range(27)]
    biases = [floats[54], floats[55]]
    camera, first = place[0], place[1]
    w_second = weights[0:64]
    spread_filters(k_one, k_two, one, two)
    last, next_ = wrapped(camera - 2), wrapped(camera + 2)
    third = wrapped(jnp.where((camera & 1) == 0, camera - 3, camera + 3))
    others = [next_, next_ ^ 1, third, last, last ^ 1]
    neighbour_features(others, pictures[...], wide, w_second, place, ids, count, offsets, right)

    zero = jnp.zeros((8 * ROWS, W), BF16)
    for block in (0, BLOCKS + 1):
        vol[block] = zero
        smooth[block] = zero[: 8 * (BAND + 2)]

    scale = jnp.float32(1.0 / 8 / 6)
    for n in range(2, 6):
        scale = jnp.where(count[0] == n, jnp.float32(1.0 / 8 / n), scale)
    swap = one_hot(iota((D, W), 0) + iota((D, W), 1) == D - 1)
    inside = iota((128, 128), 0) + iota((128, 128), 1) >= 127

    for pair in range(ROWS // 2):
        done = []
        for row in (2 * pair, 2 * pair + 1):
            upper, lower = correlated(left, right, row, upper_sum[row], lower_sum[row])
            upper = jnp.where(inside, upper * scale, 0.0)
            lower = lower * scale
            summed = jnp.concatenate(
                [
                    jnp.concatenate([jnp.zeros((128, 128), F32), upper], axis=1),
                    jnp.concatenate([jnp.where(inside, lower[:, :128], 0.0), lower[:, 128:]], axis=1),
                ],
                axis=0,
            )
            turned = pltpu.roll(summed, 1, axis=1, stride=1, stride_axis=0).astype(BF16)
            flipped = lax.dot_general(
                swap, turned, (((1,), (1,)), ((), ())), preferred_element_type=F32
            )
            done.append(flipped.reshape(BLOCKS, 8, W))
        vol[1 : BLOCKS + 1, 16 * pair : 16 * pair + 16, :] = jnp.concatenate(done, axis=1).astype(BF16)

    bias_one, bias_two = biases[0], biases[1]
    above_ok = jnp.where(first > 0, 1.0, 0.0)
    under_ok = jnp.where(first + BAND < H, 1.0, 0.0)

    for block in range(BLOCKS):
        halves = []
        for half in range(2):
            source = vol[block : block + 3, 32 * half : 32 * half + 64, :].reshape(192, W)
            total = jnp.dot(one[half, 0], source, preferred_element_type=F32)
            total = total + jnp.dot(one[half, 1], source, preferred_element_type=F32)
            halves.append(side_sum([total[40 * e : 40 * e + 40] for e in range(3)]))
        hidden = jnp.maximum(jnp.concatenate(halves, axis=0) + bias_one, 0.0)
        hidden = jnp.concatenate(
            [hidden[:8] * above_ok, hidden[8:72], hidden[72:] * under_ok], axis=0
        )
        smooth[block + 1] = hidden.astype(BF16)

    stores = []
    for block in range(BLOCKS):
        source = smooth[block : block + 3].reshape(240, W)
        total = jnp.dot(two[0], source, preferred_element_type=F32)
        total = total + jnp.dot(two[1], source, preferred_element_type=F32)
        filtered = side_sum([total[64 * e : 64 * e + 64] for e in range(3)]) + bias_two
        result[8 * block : 8 * block + 8] = filtered.reshape(8, BAND, W).astype(BF16)
        if block % 4 == 3:
            part = pl.ds(8 * block - 24, 32)
            stores.append(pltpu.make_async_copy(result.at[part], out.at[0, part], sems.at[block // 4]))
            stores[-1].start()
    for store in stores:
        store.wait()


VMEM, SMEM = pl.BlockSpec(memory_space=pltpu.VMEM), pl.BlockSpec(memory_space=pltpu.SMEM)


ANY = pl.BlockSpec(memory_space=pl.ANY)
def early_sums(table, weights, pair):
    return pl.pallas_call(
        early_kernel,
        out_shape=(
            jax.ShapeDtypeStruct((ROWS // 2, 2 * W, 128), BF16),
            jax.ShapeDtypeStruct((ROWS, 128, 128), F32),
            jax.ShapeDtypeStruct((ROWS, 128, W), F32),
            jax.ShapeDtypeStruct((64 * ROWS, TAPS), BF16),
        ),
        in_specs=[SMEM, VMEM, VMEM],
        out_specs=(VMEM,) * 4,
        scratch_shapes=[pltpu.VMEM((1, 64 * ROWS, W), BF16)],
        name="early_sums",
        cost_estimate=pl.CostEstimate(flops=2000000000, bytes_accessed=3500000, transcendentals=0),
        compiler_params=pltpu.CompilerParams(vmem_limit_bytes=16 * 1024 * 1024),
    )(table, weights, pair)


def cost_volume(table, floats, weights, pictures, sums):
    return pl.pallas_call(
        late_kernel,
        out_shape=jax.ShapeDtypeStruct((1, D, BAND, W), BF16),
        in_specs=[SMEM] * 2 + [VMEM] * 6,
        out_specs=ANY,
        scratch_shapes=[
            pltpu.VMEM((2, 2, 120, 192), BF16),
            pltpu.VMEM((2, 192, 240), BF16),
            pltpu.VMEM((5, 64 * ROWS, W), BF16),
            pltpu.VMEM((BLOCKS + 2, 8 * ROWS, W), BF16),
            pltpu.VMEM((BLOCKS + 2, 8 * (BAND + 2), W), BF16),
            pltpu.VMEM((D, BAND, W), BF16),
            pltpu.SemaphoreType.DMA((BLOCKS // 4,)),
        ],
        name="cost_volume",
        cost_estimate=pl.CostEstimate(flops=5000000000, bytes_accessed=4500000, transcendentals=0),
        compiler_params=pltpu.CompilerParams(vmem_limit_bytes=24 * 1024 * 1024),
    )(table, floats, weights, pictures, *sums)


def all_of_it(table, floats, weights, pair, before, after, far):
    sums = early_sums(table, weights, pair)
    pictures = jnp.concatenate([after, far[:1], before], axis=0)
    return cost_volume(table, floats, weights, pictures, sums)


def from_camera(value, source_of):
    return lax.ppermute(value, "cam", [(source_of(to) % CAMS, to) for to in range(CAMS)])


def on_device(
    images, neighbor_ids, neighbor_count, offsets, w_first, w_second, kernel_one, kernel_two, biases
):
    pair = jnp.concatenate([images, from_camera(images, lambda to: to ^ 1)], axis=0)
    ends = lax.axis_size("rows") - 1
    over = lax.ppermute(pair, "rows", [(i, i + 1) for i in range(ends)])
    under = lax.ppermute(pair, "rows", [(i + 1, i) for i in range(ends)])
    pair = jnp.concatenate([over[:, :, 4:], pair, under[:, :, :4]], axis=2)
    after = from_camera(pair, lambda to: to + 2)
    before = from_camera(pair, lambda to: to - 2)
    far = from_camera(pair, lambda to: to - 3 if to % 2 == 0 else to + 3)
    place = jnp.stack([lax.axis_index("cam"), lax.axis_index("rows") * BAND]).astype(jnp.int32)
    table = jnp.concatenate([place, neighbor_ids[0], offsets[0], neighbor_count])
    floats = jnp.concatenate([kernel_one, kernel_two, biases])
    weights = jnp.concatenate([w_second, jnp.pad(w_first.T, ((0, 5), (0, 0)))], axis=0)
    return all_of_it(table, floats, weights, pair, before, after, far)


def solution(mesh):
    in_specs = (
        P("cam", None, "rows", None),
        P("cam", None),
        P("cam"),
        P("cam", None),
        P(),
        P(),
        P(),
        P(),
        P(),
    )
    out_specs = P("cam", None, "rows", None)
    return jax.shard_map(
        on_device, mesh=mesh, in_specs=in_specs, out_specs=out_specs, check_vma=False
    )
```

profile of v0, /device:TPU:2, one launch (start us, length us, event | category | flops | bytes accessed | tf_op | source)
XLA Modules:
  0.0 33.4 jit_solution(12980103853959271169)
XLA Ops:
  0.0 0.0 collective-permute-start
  0.0 0.7 %fusion.1.weights = bf16[96,64]{1,0:T(8,128)(2,1)S(1)} fusion(bf16[27,64]{1,0:T(8,128)(2,1)} %bitcast.5, bf16[64,64]{1,0:T(8,128)(2,1)} %param.14), kind=kLoop, calls=%fused_computation.4 | loop fusion | flops 36864 | bytes 23936 | tf_op jit(solution)/shard_map/concatenate | solution.py:329
  0.7 0.7 %constant_dynamic-update-slice_fusion.1 = bf16[2,3,8,256]{3,2,1,0:T(8,128)(2,1)S(1)} fusion(bf16[1,3,8,256]{3,2,1,0:T(8,128)(2,1)} %param.9), kind=kLoop, calls=%fused_computation.6 | loop fusion | bytes 24576
  1.5 0.0 collective-permute-done
  1.5 4.2 %collective-permute-start.2 = (bf16[2,3,8,256]{3,2,1,0:T(8,128)(2,1)S(1)}, bf16[2,3,8,256]{3,2,1,0:T(8,128)(2,1)S(1)}, u32[]{:S(2)}, u32[]{:S(2)}) collective-permute-start(bf16[2,3,8,256]{3,2,1,0:T(8,128)(2,1)S(1)} %constant_dynamic-update-slice_fusion), channel_id=1, source_target_pairs={{1,0},{2,1},{3,2},{5,4},{6,5},{7,6},{9,8},{10,9},{11,10},{13,12},{... | collective-permute-start | bytes 73736 | tf_op jit(solution)/shard_map/ppermute | solution.py:321
  5.6 1.9 %collective-permute-start.1 = (bf16[2,3,8,256]{3,2,1,0:T(8,128)(2,1)S(1)}, bf16[2,3,8,256]{3,2,1,0:T(8,128)(2,1)S(1)}, u32[]{:S(2)}, u32[]{:S(2)}) collective-permute-start(bf16[2,3,8,256]{3,2,1,0:T(8,128)(2,1)S(1)} %constant_dynamic-update-slice_fusion), channel_id=1, source_target_pairs={{0,1},{1,2},{2,3},{4,5},{5,6},{6,7},{8,9},{9,10},{10,11},{12,13},{... | collective-permute-start | bytes 73736 | tf_op jit(solution)/shard_map/ppermute | solution.py:320
  7.6 0.8 %pad_maximum_fusion.2.floats = f32[56]{0:T(128)S(1)} fusion(f32[2]{0:T(128)} %param.17, f32[27]{0:T(128)} %param.16, f32[27]{0:T(128)} %param.15), kind=kLoop, calls=%fused_computation.7 | loop fusion | flops 112 | bytes 448 | tf_op jit(solution)/shard_map/concatenate | solution.py:328
  9.0 0.7 %concatenate.18.table = s32[15]{0:T(128)S(1)} concatenate(s32[1]{0:T(128)} %bitcast, s32[1]{0:T(128)} %bitcast.1, s32[6]{0:T(128)} %bitcast.6, s32[6]{0:T(128)} %bitcast.7, s32[1]{0:T(128)S(6)} %copy.11), dimensions={0} | concatenate | bytes 120 | tf_op jit(solution)/shard_map/concatenate | solution.py:327
  9.7 0.0 collective-permute-done.2
  9.8 1.6 %collective-permute-done.1 = bf16[2,3,8,256]{3,2,1,0:T(8,128)(2,1)S(1)} collective-permute-done((bf16[2,3,8,256]{3,2,1,0:T(8,128)(2,1)S(1)}, bf16[2,3,8,256]{3,2,1,0:T(8,128)(2,1)S(1)}, u32[]{:S(2)}, u32[]{:S(2)}) %collective-permute-start.1) | collective-permute-done | bytes 24608 | tf_op jit(solution)/shard_map/ppermute | solution.py:320
  11.4 0.1 collective-permute-start.5
  11.5 7.2 %collective-permute-start.4 = (bf16[2,3,16,256]{3,2,1,0:T(8,128)(2,1)S(1)}, bf16[2,3,16,256]{3,2,1,0:T(8,128)(2,1)S(1)}, u32[]{:S(2)}, u32[]{:S(2)}) collective-permute-start(bf16[2,3,16,256]{3,2,1,0:T(8,128)(2,1)S(1)} %pad_maximum_fusion.1.pictures), channel_id=1, source_target_pairs={{244,0},{16,4},{252,8},{24,12},{4,16},{32,20},{12,24},{40,28},{20,... | collective-permute-start | bytes 147464 | tf_op jit(solution)/shard_map/ppermute | solution.py:312
  18.7 1.3 %collective-permute-start.3 = (bf16[2,3,16,256]{3,2,1,0:T(8,128)(2,1)S(1)}, bf16[2,3,16,256]{3,2,1,0:T(8,128)(2,1)S(1)}, u32[]{:S(2)}, u32[]{:S(2)}) collective-permute-start(bf16[2,3,16,256]{3,2,1,0:T(8,128)(2,1)S(1)} %pad_maximum_fusion.1.pictures), channel_id=1, source_target_pairs={{8,0},{12,4},{16,8},{20,12},{24,16},{28,20},{32,24},{36,28},{40,32... | collective-permute-start | bytes 147464 | tf_op jit(solution)/shard_map/ppermute | solution.py:312
  20.0 1.9 %early_sums.1 = (bf16[6,512,128]{2,1,0:T(8,128)(2,1)S(1)}, f32[12,128,128]{2,1,0:T(8,128)S(1)}, f32[12,128,256]{2,1,0:T(8,128)S(1)}, bf16[768,144]{1,0:T(8,128)(2,1)S(1)}) custom-call(s32[15]{0:T(128)S(1)} %concatenate.18.table, bf16[96,64]{1,0:T(8,128)(2,1)S(1)} %fusion.1.weights, bf16[2,3,16,256]{3,2,1,0:T(8,128)(2,1)S(1)} %pad_maximum_fusion.1.pictures), custom_call_target="tpu_custom_call" | custom-call | flops 2000000000 | bytes 3500000 | tf_op jit(solution)/shard_map/early_sums/pallas_call | solution.py:267
  22.0 0.0 collective-permute-done.4
  22.0 0.0 collective-permute-done.5
  22.0 0.8 %collective-permute-done.3 = bf16[2,3,16,256]{3,2,1,0:T(8,128)(2,1)S(1)} collective-permute-done((bf16[2,3,16,256]{3,2,1,0:T(8,128)(2,1)S(1)}, bf16[2,3,16,256]{3,2,1,0:T(8,128)(2,1)S(1)}, u32[]{:S(2)}, u32[]{:S(2)}) %collective-permute-start.3) | collective-permute-done | bytes 49184 | tf_op jit(solution)/shard_map/ppermute | solution.py:312
  22.8 10.5 %cost_volume.1 = bf16[1,192,8,256]{3,2,1,0:T(8,128)(2,1)} custom-call(s32[15]{0:T(128)S(1)} %concatenate.18.table, f32[56]{0:T(128)S(1)} %pad_maximum_fusion.2.floats, bf16[96,64]{1,0:T(8,128)(2,1)S(1)} %fusion.1.weights, bf16[5,3,16,256]{3,2,1,0:T(8,128)(2,1)S(1)} %pad_maximum_fusion.pictures, bf16[6,512,128]{2,1,0:T(8,128)(2,1)S(1)} %get-tuple-element.9.left, ...), custom_call_target="tpu_custom_call" | custom-call | flops 5000000000 | bytes 4500000 | tf_op jit(solution)/shard_map/cost_volume/pallas_call | solution.py:285
  (6 shorter events, 0.1 us)
Async XLA Ops:
  0.0 1.5 %collective-permute-start = (bf16[1,3,8,256]{3,2,1,0:T(8,128)(2,1)}, bf16[1,3,8,256]{3,2,1,0:T(8,128)(2,1)S(1)}, u32[]{:S(2)}, u32[]{:S(2)}) collective-permute-start(bf16[1,3,8,256]{3,2,1,0:T(8,128)(2,1)} %param.9), channel_id=1, source_target_pairs={{4,0},{0,4},{12,8},{8,12},{20,16},{16,20},{28,24},{24,28},{36,32},... | collective-permute-start | bytes 36872 | tf_op jit(solution)/shard_map/ppermute | solution.py:312
  1.5 8.3 %collective-permute-start.2 = (bf16[2,3,8,256]{3,2,1,0:T(8,128)(2,1)S(1)}, bf16[2,3,8,256]{3,2,1,0:T(8,128)(2,1)S(1)}, u32[]{:S(2)}, u32[]{:S(2)}) collective-permute-start(bf16[2,3,8,256]{3,2,1,0:T(8,128)(2,1)S(1)} %constant_dynamic-update-slice_fusion), channel_id=1, source_target_pairs={{1,0},{2,1},{3,2},{5,4},{6,5},{7,6},{9,8},{10,9},{11,10},{13,12},{... | collective-permute-start | bytes 73736 | tf_op jit(solution)/shard_map/ppermute | solution.py:321
  5.6 5.7 %collective-permute-start.1 = (bf16[2,3,8,256]{3,2,1,0:T(8,128)(2,1)S(1)}, bf16[2,3,8,256]{3,2,1,0:T(8,128)(2,1)S(1)}, u32[]{:S(2)}, u32[]{:S(2)}) collective-permute-start(bf16[2,3,8,256]{3,2,1,0:T(8,128)(2,1)S(1)} %constant_dynamic-update-slice_fusion), channel_id=1, source_target_pairs={{0,1},{1,2},{2,3},{4,5},{5,6},{6,7},{8,9},{9,10},{10,11},{12,13},{... | collective-permute-start | bytes 73736 | tf_op jit(solution)/shard_map/ppermute | solution.py:320
  11.4 10.6 %collective-permute-start.5 = (bf16[2,3,16,256]{3,2,1,0:T(8,128)(2,1)S(1)}, bf16[2,3,16,256]{3,2,1,0:T(8,128)(2,1)S(1)}, u32[]{:S(2)}, u32[]{:S(2)}) collective-permute-start(bf16[2,3,16,256]{3,2,1,0:T(8,128)(2,1)S(1)} %pad_maximum_fusion.1.pictures), channel_id=1, source_target_pairs={{248,0},{252,4},{0,8},{4,12},{8,16},{12,20},{16,24},{20,28},{24,32... | collective-permute-start | bytes 147464 | tf_op jit(solution)/shard_map/ppermute | solution.py:312
  11.5 10.5 %collective-permute-start.4 = (bf16[2,3,16,256]{3,2,1,0:T(8,128)(2,1)S(1)}, bf16[2,3,16,256]{3,2,1,0:T(8,128)(2,1)S(1)}, u32[]{:S(2)}, u32[]{:S(2)}) collective-permute-start(bf16[2,3,16,256]{3,2,1,0:T(8,128)(2,1)S(1)} %pad_maximum_fusion.1.pictures), channel_id=1, source_target_pairs={{244,0},{16,4},{252,8},{24,12},{4,16},{32,20},{12,24},{40,28},{20,... | collective-permute-start | bytes 147464 | tf_op jit(solution)/shard_map/ppermute | solution.py:312
  18.7 4.1 %collective-permute-start.3 = (bf16[2,3,16,256]{3,2,1,0:T(8,128)(2,1)S(1)}, bf16[2,3,16,256]{3,2,1,0:T(8,128)(2,1)S(1)}, u32[]{:S(2)}, u32[]{:S(2)}) collective-permute-start(bf16[2,3,16,256]{3,2,1,0:T(8,128)(2,1)S(1)} %pad_maximum_fusion.1.pictures), channel_id=1, source_target_pairs={{8,0},{12,4},{16,8},{20,12},{24,16},{28,20},{32,24},{36,28},{40,32... | collective-permute-start | bytes 147464 | tf_op jit(solution)/shard_map/ppermute | solution.py:312
where the time goes:
time: 33.8 us; the launch traced here: 33.4 us
  starting transfers between devices  14.7 us (43%)
  Pallas kernels  12.4 us (37%)
  waiting for transfers between devices  2.39 us (7%)
  other arithmetic  1.55 us (5%)
  local copies, waits for them, and re-layouts  1.48 us (4%)
  between operations  0.9 us (3%)
    pallas_call x1, Pallas kernels, cost_volume(): pl.pallas_call(late_kernel, out_shape=jax.ShapeDtypeStruct((1, D, BAND, W...  10.5 us
    ppermute x4, starting transfers between devices, from_camera(): lax.ppermute(value, 'cam', [(source_of(to) % CAMS, to) for to in range(CA...  8.61 us
    ppermute x1, starting transfers between devices, on_device(): under = lax.ppermute(pair, 'rows', [(i + 1, i) for i in range(ends)])  4.17 us
    pallas_call x1, Pallas kernels, early_sums(): pl.pallas_call(early_kernel, out_shape=(jax.ShapeDtypeStruct((ROWS // 2,...  1.93 us
    ppermute x1, starting transfers between devices, on_device(): over = lax.ppermute(pair, 'rows', [(i, i + 1) for i in range(ends)])  1.92 us
    ppermute x1, waiting for transfers between devices, on_device(): over = lax.ppermute(pair, 'rows', [(i, i + 1) for i in range(ends)])  1.61 us
    ppermute x4, waiting for transfers between devices, from_camera(): lax.ppermute(value, 'cam', [(source_of(to) % CAMS, to) for to in range(CA...  0.78 us
    concatenate x1, other arithmetic, on_device(): floats = jnp.concatenate([kernel_one, kernel_two, biases])  0.77 us
  transfers between devices with their start and end apart: 6, of which 2 were waited for; matrix products, arithmetic and copies ran while one was open for 9% of the time, Pallas kernels for 6%

commit v1 on v0

--- a/solution.py
+++ b/solution.py
@@ -149,14 +149,11 @@
                 right[index, at : at + 64] = part.astype(BF16)
 
 
-def correlated(left, right, row, upper, lower):
-    pair, base = row // 2, W * (row % 2)
-    top = left[pair, base : base + 128]
-    bottom = left[pair, base + 128 : base + 256]
+def correlated(left, right, pair, upper, lower):
     for index in range(right.shape[0]):
         other = right[index, 128 * pair : 128 * pair + 128, :]
-        a = jnp.maximum(jnp.dot(top, other[:, 128:], preferred_element_type=F32), 0.0)
-        b = jnp.maximum(jnp.dot(bottom, other, preferred_element_type=F32), 0.0)
+        a = jnp.maximum(jnp.dot(left[pair, 0:256], other[:, 128:], preferred_element_type=F32), 0.0)
+        b = jnp.maximum(jnp.dot(left[pair, 256:512], other, preferred_element_type=F32), 0.0)
         upper = a if upper is None else upper + a
         lower = b if lower is None else lower + b
     return upper, lower
@@ -172,13 +169,16 @@
         found = features(columns, wide, w_second, group, place[1] - 2, True)
         for half in range(2):
             pair = jnp.concatenate(found[2 * half : 2 * half + 2], axis=0).T
-            left[2 * group + half, 0:W] = jnp.where(lane < 64, pair, 0.0).astype(BF16)
-            left[2 * group + half, W : 2 * W] = jnp.where(lane >= 64, pair, 0.0).astype(BF16)
+            one_row = jnp.where(lane < 64, pair, 0.0).astype(BF16)
+            next_row = jnp.where(lane >= 64, pair, 0.0).astype(BF16)
+            at = 2 * group + half
+            left[at, 0:128], left[at, 128:256] = one_row[:128], next_row[:128]
+            left[at, 256:384], left[at, 384:512] = one_row[128:], next_row[128:]
     neighbour_features(
         [place[0] ^ 1], pictures[1], wide, w_second, place, ids, count, offsets, right
     )
-    for row in range(ROWS):
-        upper[row], lower[row] = correlated(left, right, row, None, None)
+    for pair in range(ROWS // 2):
+        upper[pair], lower[pair] = correlated(left, right, pair, None, None)
 
 
 def late_kernel(
@@ -209,8 +209,9 @@
 
     for pair in range(ROWS // 2):
         done = []
-        for row in (2 * pair, 2 * pair + 1):
-            upper, lower = correlated(left, right, row, upper_sum[row], lower_sum[row])
+        uppers, lowers = correlated(left, right, pair, upper_sum[pair], lower_sum[pair])
+        for row in range(2):
+            upper, lower = uppers[128 * row : 128 * row + 128], lowers[128 * row : 128 * row + 128]
             upper = jnp.where(inside, upper * scale, 0.0)
             lower = lower * scale
             summed = jnp.concatenate(
@@ -268,8 +269,8 @@
         early_kernel,
         out_shape=(
             jax.ShapeDtypeStruct((ROWS // 2, 2 * W, 128), BF16),
-            jax.ShapeDtypeStruct((ROWS, 128, 128), F32),
-            jax.ShapeDtypeStruct((ROWS, 128, W), F32),
+            jax.ShapeDtypeStruct((ROWS // 2, 256, 128), F32),
+            jax.ShapeDtypeStruct((ROWS // 2, 256, W), F32),
             jax.ShapeDtypeStruct((64 * ROWS, TAPS), BF16),
         ),
         in_specs=[SMEM, VMEM, VMEM],

time: 33.8 us -> 32.7 us (0.967)
  Pallas kernels: 12.4 us -> 11.4 us
    pallas_call x1, Pallas kernels: 10.5 us -> 9.34 us  [cost_volume(): pl.pallas_call(late_kernel, out_shape=jax.ShapeDtypeStruct((1, D, BAND, W...]
where the time goes in v1:
time: 32.7 us; the launch traced here: 32.3 us
  starting transfers between devices  14.7 us (45%)
  Pallas kernels  11.4 us (35%)
  waiting for transfers between devices  2.26 us (7%)
  other arithmetic  1.55 us (5%)
  local copies, waits for them, and re-layouts  1.48 us (5%)
  between operations  0.9 us (3%)
    pallas_call x1, Pallas kernels, cost_volume(): pl.pallas_call(late_kernel, out_shape=jax.ShapeDtypeStruct((1, D, BAND, W...  9.34 us
    ppermute x4, starting transfers between devices, from_camera(): lax.ppermute(value, 'cam', [(source_of(to) % CAMS, to) for to in range(CA...  8.61 us
    ppermute x1, starting transfers between devices, on_device(): under = lax.ppermute(pair, 'rows', [(i + 1, i) for i in range(ends)])  4.17 us
    pallas_call x1, Pallas kernels, early_sums(): pl.pallas_call(early_kernel, out_shape=(jax.ShapeDtypeStruct((ROWS // 2,...  2.06 us
    ppermute x1, starting transfers between devices, on_device(): over = lax.ppermute(pair, 'rows', [(i, i + 1) for i in range(ends)])  1.92 us
    ppermute x1, waiting for transfers between devices, on_device(): over = lax.ppermute(pair, 'rows', [(i, i + 1) for i in range(ends)])  1.61 us
    concatenate x1, other arithmetic, on_device(): floats = jnp.concatenate([kernel_one, kernel_two, biases])  0.77 us
    concatenate x1, local copies, waits for them, and re-layouts, on_device(): jnp.concatenate([place, neighbor_ids[0], offsets[0], neighbor_count])  0.75 us
  transfers between devices with their start and end apart: 6, of which 2 were waited for; matrix products, arithmetic and copies ran while one was open for 9% of the time, Pallas kernels for 6%

profile of v1, /device:TPU:2, one launch (start us, length us, event | category | flops | bytes accessed | tf_op | source)
XLA Modules:
  0.0 32.3 jit_solution(16334171980506805173)
XLA Ops:
  0.0 0.0 collective-permute-start
  0.0 0.7 %fusion.1.weights = bf16[96,64]{1,0:T(8,128)(2,1)S(1)} fusion(bf16[27,64]{1,0:T(8,128)(2,1)} %bitcast.5, bf16[64,64]{1,0:T(8,128)(2,1)} %param.14), kind=kLoop, calls=%fused_computation.4 | loop fusion | flops 36864 | bytes 23936 | tf_op jit(solution)/shard_map/concatenate | solution.py:330
  0.7 0.7 %constant_dynamic-update-slice_fusion.1 = bf16[2,3,8,256]{3,2,1,0:T(8,128)(2,1)S(1)} fusion(bf16[1,3,8,256]{3,2,1,0:T(8,128)(2,1)} %param.9), kind=kLoop, calls=%fused_computation.6 | loop fusion | bytes 24576
  1.5 0.0 collective-permute-done
  1.5 4.2 %collective-permute-start.2 = (bf16[2,3,8,256]{3,2,1,0:T(8,128)(2,1)S(1)}, bf16[2,3,8,256]{3,2,1,0:T(8,128)(2,1)S(1)}, u32[]{:S(2)}, u32[]{:S(2)}) collective-permute-start(bf16[2,3,8,256]{3,2,1,0:T(8,128)(2,1)S(1)} %constant_dynamic-update-slice_fusion), channel_id=1, source_target_pairs={{1,0},{2,1},{3,2},{5,4},{6,5},{7,6},{9,8},{10,9},{11,10},{13,12},{... | collective-permute-start | bytes 73736 | tf_op jit(solution)/shard_map/ppermute | solution.py:322
  5.6 1.9 %collective-permute-start.1 = (bf16[2,3,8,256]{3,2,1,0:T(8,128)(2,1)S(1)}, bf16[2,3,8,256]{3,2,1,0:T(8,128)(2,1)S(1)}, u32[]{:S(2)}, u32[]{:S(2)}) collective-permute-start(bf16[2,3,8,256]{3,2,1,0:T(8,128)(2,1)S(1)} %constant_dynamic-update-slice_fusion), channel_id=1, source_target_pairs={{0,1},{1,2},{2,3},{4,5},{5,6},{6,7},{8,9},{9,10},{10,11},{12,13},{... | collective-permute-start | bytes 73736 | tf_op jit(solution)/shard_map/ppermute | solution.py:321
  7.6 0.8 %pad_maximum_fusion.2.floats = f32[56]{0:T(128)S(1)} fusion(f32[2]{0:T(128)} %param.17, f32[27]{0:T(128)} %param.16, f32[27]{0:T(128)} %param.15), kind=kLoop, calls=%fused_computation.7 | loop fusion | flops 112 | bytes 448 | tf_op jit(solution)/shard_map/concatenate | solution.py:329
  9.0 0.7 %concatenate.18.table = s32[15]{0:T(128)S(1)} concatenate(s32[1]{0:T(128)} %bitcast, s32[1]{0:T(128)} %bitcast.1, s32[6]{0:T(128)} %bitcast.6, s32[6]{0:T(128)} %bitcast.7, s32[1]{0:T(128)S(6)} %copy.11), dimensions={0} | concatenate | bytes 120 | tf_op jit(solution)/shard_map/concatenate | solution.py:328
  9.7 0.0 collective-permute-done.2
  9.8 1.6 %collective-permute-done.1 = bf16[2,3,8,256]{3,2,1,0:T(8,128)(2,1)S(1)} collective-permute-done((bf16[2,3,8,256]{3,2,1,0:T(8,128)(2,1)S(1)}, bf16[2,3,8,256]{3,2,1,0:T(8,128)(2,1)S(1)}, u32[]{:S(2)}, u32[]{:S(2)}) %collective-permute-start.1) | collective-permute-done | bytes 24608 | tf_op jit(solution)/shard_map/ppermute | solution.py:321
  11.4 0.1 collective-permute-start.5
  11.5 7.2 %collective-permute-start.4 = (bf16[2,3,16,256]{3,2,1,0:T(8,128)(2,1)S(1)}, bf16[2,3,16,256]{3,2,1,0:T(8,128)(2,1)S(1)}, u32[]{:S(2)}, u32[]{:S(2)}) collective-permute-start(bf16[2,3,16,256]{3,2,1,0:T(8,128)(2,1)S(1)} %pad_maximum_fusion.1.pictures), channel_id=1, source_target_pairs={{244,0},{16,4},{252,8},{24,12},{4,16},{32,20},{12,24},{40,28},{20,... | collective-permute-start | bytes 147464 | tf_op jit(solution)/shard_map/ppermute | solution.py:313
  18.7 1.3 %collective-permute-start.3 = (bf16[2,3,16,256]{3,2,1,0:T(8,128)(2,1)S(1)}, bf16[2,3,16,256]{3,2,1,0:T(8,128)(2,1)S(1)}, u32[]{:S(2)}, u32[]{:S(2)}) collective-permute-start(bf16[2,3,16,256]{3,2,1,0:T(8,128)(2,1)S(1)} %pad_maximum_fusion.1.pictures), channel_id=1, source_target_pairs={{8,0},{12,4},{16,8},{20,12},{24,16},{28,20},{32,24},{36,28},{40,32... | collective-permute-start | bytes 147464 | tf_op jit(solution)/shard_map/ppermute | solution.py:313
  20.0 2.1 %early_sums.1 = (bf16[6,512,128]{2,1,0:T(8,128)(2,1)S(1)}, f32[6,256,128]{2,1,0:T(8,128)S(1)}, f32[6,256,256]{2,1,0:T(8,128)S(1)}, bf16[768,144]{1,0:T(8,128)(2,1)S(1)}) custom-call(s32[15]{0:T(128)S(1)} %concatenate.18.table, bf16[96,64]{1,0:T(8,128)(2,1)S(1)} %fusion.1.weights, bf16[2,3,16,256]{3,2,1,0:T(8,128)(2,1)S(1)} %pad_maximum_fusion.1.pictures), custom_call_target="tpu_custom_call" | custom-call | flops 2000000000 | bytes 3500000 | tf_op jit(solution)/shard_map/early_sums/pallas_call | solution.py:268
  22.1 0.0 collective-permute-done.4
  22.1 0.0 collective-permute-done.5
  22.1 0.6 %collective-permute-done.3 = bf16[2,3,16,256]{3,2,1,0:T(8,128)(2,1)S(1)} collective-permute-done((bf16[2,3,16,256]{3,2,1,0:T(8,128)(2,1)S(1)}, bf16[2,3,16,256]{3,2,1,0:T(8,128)(2,1)S(1)}, u32[]{:S(2)}, u32[]{:S(2)}) %collective-permute-start.3) | collective-permute-done | bytes 49184 | tf_op jit(solution)/shard_map/ppermute | solution.py:313
  22.8 9.3 %cost_volume.1 = bf16[1,192,8,256]{3,2,1,0:T(8,128)(2,1)} custom-call(s32[15]{0:T(128)S(1)} %concatenate.18.table, f32[56]{0:T(128)S(1)} %pad_maximum_fusion.2.floats, bf16[96,64]{1,0:T(8,128)(2,1)S(1)} %fusion.1.weights, bf16[5,3,16,256]{3,2,1,0:T(8,128)(2,1)S(1)} %pad_maximum_fusion.pictures, bf16[6,512,128]{2,1,0:T(8,128)(2,1)S(1)} %get-tuple-element.9.left, ...), custom_call_target="tpu_custom_call" | custom-call | flops 5000000000 | bytes 4500000 | tf_op jit(solution)/shard_map/cost_volume/pallas_call | solution.py:286
  (6 shorter events, 0.1 us)
Async XLA Ops:
  0.0 1.5 %collective-permute-start = (bf16[1,3,8,256]{3,2,1,0:T(8,128)(2,1)}, bf16[1,3,8,256]{3,2,1,0:T(8,128)(2,1)S(1)}, u32[]{:S(2)}, u32[]{:S(2)}) collective-permute-start(bf16[1,3,8,256]{3,2,1,0:T(8,128)(2,1)} %param.9), channel_id=1, source_target_pairs={{4,0},{0,4},{12,8},{8,12},{20,16},{16,20},{28,24},{24,28},{36,32},... | collective-permute-start | bytes 36872 | tf_op jit(solution)/shard_map/ppermute | solution.py:313
  1.5 8.3 %collective-permute-start.2 = (bf16[2,3,8,256]{3,2,1,0:T(8,128)(2,1)S(1)}, bf16[2,3,8,256]{3,2,1,0:T(8,128)(2,1)S(1)}, u32[]{:S(2)}, u32[]{:S(2)}) collective-permute-start(bf16[2,3,8,256]{3,2,1,0:T(8,128)(2,1)S(1)} %constant_dynamic-update-slice_fusion), channel_id=1, source_target_pairs={{1,0},{2,1},{3,2},{5,4},{6,5},{7,6},{9,8},{10,9},{11,10},{13,12},{... | collective-permute-start | bytes 73736 | tf_op jit(solution)/shard_map/ppermute | solution.py:322
  5.6 5.7 %collective-permute-start.1 = (bf16[2,3,8,256]{3,2,1,0:T(8,128)(2,1)S(1)}, bf16[2,3,8,256]{3,2,1,0:T(8,128)(2,1)S(1)}, u32[]{:S(2)}, u32[]{:S(2)}) collective-permute-start(bf16[2,3,8,256]{3,2,1,0:T(8,128)(2,1)S(1)} %constant_dynamic-update-slice_fusion), channel_id=1, source_target_pairs={{0,1},{1,2},{2,3},{4,5},{5,6},{6,7},{8,9},{9,10},{10,11},{12,13},{... | collective-permute-start | bytes 73736 | tf_op jit(solution)/shard_map/ppermute | solution.py:321
  11.4 10.7 %collective-permute-start.5 = (bf16[2,3,16,256]{3,2,1,0:T(8,128)(2,1)S(1)}, bf16[2,3,16,256]{3,2,1,0:T(8,128)(2,1)S(1)}, u32[]{:S(2)}, u32[]{:S(2)}) collective-permute-start(bf16[2,3,16,256]{3,2,1,0:T(8,128)(2,1)S(1)} %pad_maximum_fusion.1.pictures), channel_id=1, source_target_pairs={{248,0},{252,4},{0,8},{4,12},{8,16},{12,20},{16,24},{20,28},{24,32... | collective-permute-start | bytes 147464 | tf_op jit(solution)/shard_map/ppermute | solution.py:313
  11.5 10.6 %collective-permute-start.4 = (bf16[2,3,16,256]{3,2,1,0:T(8,128)(2,1)S(1)}, bf16[2,3,16,256]{3,2,1,0:T(8,128)(2,1)S(1)}, u32[]{:S(2)}, u32[]{:S(2)}) collective-permute-start(bf16[2,3,16,256]{3,2,1,0:T(8,128)(2,1)S(1)} %pad_maximum_fusion.1.pictures), channel_id=1, source_target_pairs={{244,0},{16,4},{252,8},{24,12},{4,16},{32,20},{12,24},{40,28},{20,... | collective-permute-start | bytes 147464 | tf_op jit(solution)/shard_map/ppermute | solution.py:313
  18.7 4.1 %collective-permute-start.3 = (bf16[2,3,16,256]{3,2,1,0:T(8,128)(2,1)S(1)}, bf16[2,3,16,256]{3,2,1,0:T(8,128)(2,1)S(1)}, u32[]{:S(2)}, u32[]{:S(2)}) collective-permute-start(bf16[2,3,16,256]{3,2,1,0:T(8,128)(2,1)S(1)} %pad_maximum_fusion.1.pictures), channel_id=1, source_target_pairs={{8,0},{12,4},{16,8},{20,12},{24,16},{28,20},{32,24},{36,28},{40,32... | collective-permute-start | bytes 147464 | tf_op jit(solution)/shard_map/ppermute | solution.py:313

commit v2 on v1

--- a/solution.py
+++ b/solution.py
@@ -159,7 +159,10 @@
     return upper, lower
 
 
-def early_kernel(table, weights, pictures, left, upper, lower, wide, right):
+def early_kernel(table, floats, weights, pictures, left, upper, lower, wide, one, two, right):
+    k_one = [floats[n] for n in range(27)]
+    k_two = [floats[27 + n] for n in range(27)]
+    spread_filters(k_one, k_two, one, two)
     place, ids, count, offsets = read_table(table)
     columns = columns_of(lambda p: pictures[0, p], None)
     w_second = weights[0:64]
@@ -182,15 +185,12 @@
 
 
 def late_kernel(
-    table, floats, weights, pictures, left, upper_sum, lower_sum, wide, out, one, two, right, vol, smooth, result, sems
+    table, floats, weights, pictures, left, upper_sum, lower_sum, wide, one, two, out, right, vol, smooth, result, sems
 ):
     place, ids, count, offsets = read_table(table)
-    k_one = [floats[n] for n in range(27)]
-    k_two = [floats[27 + n] for n in range(27)]
     biases = [floats[54], floats[55]]
     camera, first = place[0], place[1]
     w_second = weights[0:64]
-    spread_filters(k_one, k_two, one, two)
     last, next_ = wrapped(camera - 2), wrapped(camera + 2)
     third = wrapped(jnp.where((camera & 1) == 0, camera - 3, camera + 3))
     others = [next_, next_ ^ 1, third, last, last ^ 1]
@@ -264,7 +264,7 @@
 
 
 ANY = pl.BlockSpec(memory_space=pl.ANY)
-def early_sums(table, weights, pair):
+def early_sums(table, floats, weights, pair):
     return pl.pallas_call(
         early_kernel,
         out_shape=(
@@ -272,25 +272,25 @@
             jax.ShapeDtypeStruct((ROWS // 2, 256, 128), F32),
             jax.ShapeDtypeStruct((ROWS // 2, 256, W), F32),
             jax.ShapeDtypeStruct((64 * ROWS, TAPS), BF16),
+            jax.ShapeDtypeStruct((2, 2, 120, 192), BF16),
+            jax.ShapeDtypeStruct((2, 192, 240), BF16),
         ),
-        in_specs=[SMEM, VMEM, VMEM],
-        out_specs=(VMEM,) * 4,
+        in_specs=[SMEM, SMEM, VMEM, VMEM],
+        out_specs=(VMEM,) * 6,
         scratch_shapes=[pltpu.VMEM((1, 64 * ROWS, W), BF16)],
         name="early_sums",
         cost_estimate=pl.CostEstimate(flops=2000000000, bytes_accessed=3500000, transcendentals=0),
         compiler_params=pltpu.CompilerParams(vmem_limit_bytes=16 * 1024 * 1024),
-    )(table, weights, pair)
+    )(table, floats, weights, pair)
 
 
 def cost_volume(table, floats, weights, pictures, sums):
     return pl.pallas_call(
         late_kernel,
         out_shape=jax.ShapeDtypeStruct((1, D, BAND, W), BF16),
-        in_specs=[SMEM] * 2 + [VMEM] * 6,
+        in_specs=[SMEM] * 2 + [VMEM] * 8,
         out_specs=ANY,
         scratch_shapes=[
-            pltpu.VMEM((2, 2, 120, 192), BF16),
-            pltpu.VMEM((2, 192, 240), BF16),
             pltpu.VMEM((5, 64 * ROWS, W), BF16),
             pltpu.VMEM((BLOCKS + 2, 8 * ROWS, W), BF16),
             pltpu.VMEM((BLOCKS + 2, 8 * (BAND + 2), W), BF16),
@@ -304,7 +304,7 @@
 
 
 def all_of_it(table, floats, weights, pair, before, after, far):
-    sums = early_sums(table, weights, pair)
+    sums = early_sums(table, floats, weights, pair)
     pictures = jnp.concatenate([after, far[:1], before], axis=0)
     return cost_volume(table, floats, weights, pictures, sums)
 

time: 32.7 us -> 32.4 us (level)
  waiting for transfers between devices: 2.26 us -> 1.92 us
    ppermute x4, waiting for transfers between devices: 0.65 us -> 0.31 us  [from_camera(): lax.ppermute(value, 'cam', [(source_of(to) % CAMS, to) for to in range(CA...]
    pallas_call x1, Pallas kernels: 2.06 us -> 2.4 us  [early_sums(): pl.pallas_call(early_kernel, out_shape=(jax.ShapeDtypeStruct((ROWS // 2,...]
  transfers between devices with their start and end apart: 6 -> 6, of which waited for: 2 -> 2; matrix products, arithmetic and copies ran while one was open for 9% -> 9% of each run, Pallas kernels for 6% -> 7%
where the time goes in v2:
time: 32.4 us; the launch traced here: 32 us
  starting transfers between devices  14.7 us (45%)
  Pallas kernels  11.5 us (35%)
  waiting for transfers between devices  1.92 us (6%)
  other arithmetic  1.55 us (5%)
  local copies, waits for them, and re-layouts  1.48 us (5%)
  between operations  0.9 us (3%)
    pallas_call x1, Pallas kernels, cost_volume(): pl.pallas_call(late_kernel, out_shape=jax.ShapeDtypeStruct((1, D, BAND, W...  9.08 us
    ppermute x4, starting transfers between devices, from_camera(): lax.ppermute(value, 'cam', [(source_of(to) % CAMS, to) for to in range(CA...  8.61 us
    ppermute x1, starting transfers between devices, on_device(): under = lax.ppermute(pair, 'rows', [(i + 1, i) for i in range(ends)])  4.17 us
    pallas_call x1, Pallas kernels, early_sums(): pl.pallas_call(early_kernel, out_shape=(jax.ShapeDtypeStruct((ROWS // 2,...  2.4 us
    ppermute x1, starting transfers between devices, on_device(): over = lax.ppermute(pair, 'rows', [(i, i + 1) for i in range(ends)])  1.92 us
    ppermute x1, waiting for transfers between devices, on_device(): over = lax.ppermute(pair, 'rows', [(i, i + 1) for i in range(ends)])  1.61 us
    concatenate x1, other arithmetic, on_device(): floats = jnp.concatenate([kernel_one, kernel_two, biases])  0.77 us
    concatenate x1, local copies, waits for them, and re-layouts, on_device(): jnp.concatenate([place, neighbor_ids[0], offsets[0], neighbor_count])  0.75 us
  transfers between devices with their start and end apart: 6, of which 2 were waited for; matrix products, arithmetic and copies ran while one was open for 9% of the time, Pallas kernels for 7%

profile of v2, /device:TPU:2, one launch (start us, length us, event | category | flops | bytes accessed | tf_op | source)
XLA Modules:
  0.0 32.0 jit_solution(10024039707404827003)
XLA Ops:
  0.0 0.0 collective-permute-start
  0.0 0.7 %fusion.1.weights = bf16[96,64]{1,0:T(8,128)(2,1)S(1)} fusion(bf16[27,64]{1,0:T(8,128)(2,1)} %bitcast.5, bf16[64,64]{1,0:T(8,128)(2,1)} %param.14), kind=kLoop, calls=%fused_computation.4 | loop fusion | flops 36864 | bytes 23936 | tf_op jit(solution)/shard_map/concatenate | solution.py:330
  0.7 0.7 %constant_dynamic-update-slice_fusion.1 = bf16[2,3,8,256]{3,2,1,0:T(8,128)(2,1)S(1)} fusion(bf16[1,3,8,256]{3,2,1,0:T(8,128)(2,1)} %param.9), kind=kLoop, calls=%fused_computation.6 | loop fusion | bytes 24576
  1.5 0.0 collective-permute-done
  1.5 4.2 %collective-permute-start.2 = (bf16[2,3,8,256]{3,2,1,0:T(8,128)(2,1)S(1)}, bf16[2,3,8,256]{3,2,1,0:T(8,128)(2,1)S(1)}, u32[]{:S(2)}, u32[]{:S(2)}) collective-permute-start(bf16[2,3,8,256]{3,2,1,0:T(8,128)(2,1)S(1)} %constant_dynamic-update-slice_fusion), channel_id=1, source_target_pairs={{1,0},{2,1},{3,2},{5,4},{6,5},{7,6},{9,8},{10,9},{11,10},{13,12},{... | collective-permute-start | bytes 73736 | tf_op jit(solution)/shard_map/ppermute | solution.py:322
  5.6 1.9 %collective-permute-start.1 = (bf16[2,3,8,256]{3,2,1,0:T(8,128)(2,1)S(1)}, bf16[2,3,8,256]{3,2,1,0:T(8,128)(2,1)S(1)}, u32[]{:S(2)}, u32[]{:S(2)}) collective-permute-start(bf16[2,3,8,256]{3,2,1,0:T(8,128)(2,1)S(1)} %constant_dynamic-update-slice_fusion), channel_id=1, source_target_pairs={{0,1},{1,2},{2,3},{4,5},{5,6},{6,7},{8,9},{9,10},{10,11},{12,13},{... | collective-permute-start | bytes 73736 | tf_op jit(solution)/shard_map/ppermute | solution.py:321
  7.6 0.8 %pad_maximum_fusion.2.floats = f32[56]{0:T(128)S(1)} fusion(f32[2]{0:T(128)} %param.17, f32[27]{0:T(128)} %param.16, f32[27]{0:T(128)} %param.15), kind=kLoop, calls=%fused_computation.7 | loop fusion | flops 112 | bytes 448 | tf_op jit(solution)/shard_map/concatenate | solution.py:329
  9.0 0.7 %concatenate.18.table = s32[15]{0:T(128)S(1)} concatenate(s32[1]{0:T(128)} %bitcast, s32[1]{0:T(128)} %bitcast.1, s32[6]{0:T(128)} %bitcast.6, s32[6]{0:T(128)} %bitcast.7, s32[1]{0:T(128)S(6)} %copy.11), dimensions={0} | concatenate | bytes 120 | tf_op jit(solution)/shard_map/concatenate | solution.py:328
  9.7 0.0 collective-permute-done.2
  9.8 1.6 %collective-permute-done.1 = bf16[2,3,8,256]{3,2,1,0:T(8,128)(2,1)S(1)} collective-permute-done((bf16[2,3,8,256]{3,2,1,0:T(8,128)(2,1)S(1)}, bf16[2,3,8,256]{3,2,1,0:T(8,128)(2,1)S(1)}, u32[]{:S(2)}, u32[]{:S(2)}) %collective-permute-start.1) | collective-permute-done | bytes 24608 | tf_op jit(solution)/shard_map/ppermute | solution.py:321
  11.4 0.1 collective-permute-start.5
  11.5 7.2 %collective-permute-start.4 = (bf16[2,3,16,256]{3,2,1,0:T(8,128)(2,1)S(1)}, bf16[2,3,16,256]{3,2,1,0:T(8,128)(2,1)S(1)}, u32[]{:S(2)}, u32[]{:S(2)}) collective-permute-start(bf16[2,3,16,256]{3,2,1,0:T(8,128)(2,1)S(1)} %pad_maximum_fusion.1.pictures), channel_id=1, source_target_pairs={{244,0},{16,4},{252,8},{24,12},{4,16},{32,20},{12,24},{40,28},{20,... | collective-permute-start | bytes 147464 | tf_op jit(solution)/shard_map/ppermute | solution.py:313
  18.7 1.3 %collective-permute-start.3 = (bf16[2,3,16,256]{3,2,1,0:T(8,128)(2,1)S(1)}, bf16[2,3,16,256]{3,2,1,0:T(8,128)(2,1)S(1)}, u32[]{:S(2)}, u32[]{:S(2)}) collective-permute-start(bf16[2,3,16,256]{3,2,1,0:T(8,128)(2,1)S(1)} %pad_maximum_fusion.1.pictures), channel_id=1, source_target_pairs={{8,0},{12,4},{16,8},{20,12},{24,16},{28,20},{32,24},{36,28},{40,32... | collective-permute-start | bytes 147464 | tf_op jit(solution)/shard_map/ppermute | solution.py:313
  20.0 2.4 %early_sums.1 = (bf16[6,512,128]{2,1,0:T(8,128)(2,1)S(1)}, f32[6,256,128]{2,1,0:T(8,128)S(1)}, f32[6,256,256]{2,1,0:T(8,128)S(1)}, bf16[768,144]{1,0:T(8,128)(2,...) custom-call(s32[15]{0:T(128)S(1)} %concatenate.18.table, f32[56]{0:T(128)S(1)} %pad_maximum_fusion.2.floats, ...), custom_call_target="tpu_custom_call" | custom-call | flops 2000000000 | bytes 3500000 | tf_op jit(solution)/shard_map/early_sums/pallas_call | solution.py:268
  22.4 0.0 collective-permute-done.4
  22.5 0.0 collective-permute-done.5
  22.5 0.3 collective-permute-done.3
  22.8 9.1 %cost_volume.1 = bf16[1,192,8,256]{3,2,1,0:T(8,128)(2,1)} custom-call(s32[15]{0:T(128)S(1)} %concatenate.18.table, f32[56]{0:T(128)S(1)} %pad_maximum_fusion.2.floats, bf16[96,64]{1,0:T(8,128)(2,1)S(1)} %fusion.1.weights, bf16[5,3,16,256]{3,2,1,0:T(8,128)(2,1)S(1)} %pad_maximum_fusion.pictures, bf16[6,512,128]{2,1,0:T(8,128)(2,1)S(1)} %get-tuple-element.11.left, ...), custom_call_target="tpu_custom_call" | custom-call | flops 5000000000 | bytes 4500000 | tf_op jit(solution)/shard_map/cost_volume/pallas_call | solution.py:288
  (6 shorter events, 0.1 us)
Async XLA Ops:
  0.0 1.5 %collective-permute-start = (bf16[1,3,8,256]{3,2,1,0:T(8,128)(2,1)}, bf16[1,3,8,256]{3,2,1,0:T(8,128)(2,1)S(1)}, u32[]{:S(2)}, u32[]{:S(2)}) collective-permute-start(bf16[1,3,8,256]{3,2,1,0:T(8,128)(2,1)} %param.9), channel_id=1, source_target_pairs={{4,0},{0,4},{12,8},{8,12},{20,16},{16,20},{28,24},{24,28},{36,32},... | collective-permute-start | bytes 36872 | tf_op jit(solution)/shard_map/ppermute | solution.py:313
  1.5 8.3 %collective-permute-start.2 = (bf16[2,3,8,256]{3,2,1,0:T(8,128)(2,1)S(1)}, bf16[2,3,8,256]{3,2,1,0:T(8,128)(2,1)S(1)}, u32[]{:S(2)}, u32[]{:S(2)}) collective-permute-start(bf16[2,3,8,256]{3,2,1,0:T(8,128)(2,1)S(1)} %constant_dynamic-update-slice_fusion), channel_id=1, source_target_pairs={{1,0},{2,1},{3,2},{5,4},{6,5},{7,6},{9,8},{10,9},{11,10},{13,12},{... | collective-permute-start | bytes 73736 | tf_op jit(solution)/shard_map/ppermute | solution.py:322
  5.6 5.7 %collective-permute-start.1 = (bf16[2,3,8,256]{3,2,1,0:T(8,128)(2,1)S(1)}, bf16[2,3,8,256]{3,2,1,0:T(8,128)(2,1)S(1)}, u32[]{:S(2)}, u32[]{:S(2)}) collective-permute-start(bf16[2,3,8,256]{3,2,1,0:T(8,128)(2,1)S(1)} %constant_dynamic-update-slice_fusion), channel_id=1, source_target_pairs={{0,1},{1,2},{2,3},{4,5},{5,6},{6,7},{8,9},{9,10},{10,11},{12,13},{... | collective-permute-start | bytes 73736 | tf_op jit(solution)/shard_map/ppermute | solution.py:321
  11.4 11.1 %collective-permute-start.5 = (bf16[2,3,16,256]{3,2,1,0:T(8,128)(2,1)S(1)}, bf16[2,3,16,256]{3,2,1,0:T(8,128)(2,1)S(1)}, u32[]{:S(2)}, u32[]{:S(2)}) collective-permute-start(bf16[2,3,16,256]{3,2,1,0:T(8,128)(2,1)S(1)} %pad_maximum_fusion.1.pictures), channel_id=1, source_target_pairs={{248,0},{252,4},{0,8},{4,12},{8,16},{12,20},{16,24},{20,28},{24,32... | collective-permute-start | bytes 147464 | tf_op jit(solution)/shard_map/ppermute | solution.py:313
  11.5 10.9 %collective-permute-start.4 = (bf16[2,3,16,256]{3,2,1,0:T(8,128)(2,1)S(1)}, bf16[2,3,16,256]{3,2,1,0:T(8,128)(2,1)S(1)}, u32[]{:S(2)}, u32[]{:S(2)}) collective-permute-start(bf16[2,3,16,256]{3,2,1,0:T(8,128)(2,1)S(1)} %pad_maximum_fusion.1.pictures), channel_id=1, source_target_pairs={{244,0},{16,4},{252,8},{24,12},{4,16},{32,20},{12,24},{40,28},{20,... | collective-permute-start | bytes 147464 | tf_op jit(solution)/shard_map/ppermute | solution.py:313
  18.7 4.1 %collective-permute-start.3 = (bf16[2,3,16,256]{3,2,1,0:T(8,128)(2,1)S(1)}, bf16[2,3,16,256]{3,2,1,0:T(8,128)(2,1)S(1)}, u32[]{:S(2)}, u32[]{:S(2)}) collective-permute-start(bf16[2,3,16,256]{3,2,1,0:T(8,128)(2,1)S(1)} %pad_maximum_fusion.1.pictures), channel_id=1, source_target_pairs={{8,0},{12,4},{16,8},{20,12},{24,16},{28,20},{32,24},{36,28},{40,32... | collective-permute-start | bytes 147464 | tf_op jit(solution)/shard_map/ppermute | solution.py:313
